TPU v7x, 256 devices: a whole 4x4x8 slice. The times are simulated.
256 devices in a mesh: rows: 64 (over x, z, core), rhs: 4 (over y).
Axes of the slice: x: 4, y: 4, z: 8, core: 2. Of those that a mesh axis runs over, the one named last changes fastest.
Arguments:
- factor: float32 [12288, 12288], P('rows', 'rhs'), may hold values from -0.1 to 0.1
- pattern: int32 [192, 192], P('rows'), may hold values 0 or 1
- owner: int32 [192], P('rows'), may hold values from 0 to 191, each once
- right_side: float32 [64, 12288], P('rhs', 'rows'), may hold values from -6 to 6
Outputs:
- solution: float32 [64, 12288], P('rhs', 'rows')
All inputs are finite; a program needn't handle non-finite values. No bound on the sum of `pattern` on one device may be relied on, other than what follows from the above.
Results may differ from a plain program's by a relative error of at most 0.0001.
Values sent between devices are 32-bit elements; how exact they have to be, the bound alone decides.
No kernel may reach another device: no remote copies, remote signals or barrier semaphores. Data moves between devices by JAX's collectives and lax.ppermute only.
A program may use at most 192 MiB of HBM per device.

v0:
```python
import jax
import jax.numpy as jnp
from jax import lax
from jax.sharding import PartitionSpec as P


def classify(ids, leaf):
    level = jnp.where(ids < 4 * leaf, 2, jnp.where(ids < 8 * leaf, 1, 0)).astype(jnp.int32)
    group = jnp.where(
        level == 2, ids // leaf, jnp.where(level == 1, (ids - 4 * leaf) // (2 * leaf), 0)
    )
    return (level, group)


def reorder(vectors, index, block):
    count = vectors.shape[0]
    return jnp.take(vectors.reshape(count, -1, block), index, axis=1).reshape(count, -1)


def times_rows(vectors, matrix):
    return lax.dot_general(
        vectors, matrix, (((1,), (1,)), ((), ())), precision=lax.Precision.HIGHEST
    )


def times_cols(vectors, matrix):
    return jnp.dot(vectors, matrix, precision=lax.Precision.HIGHEST)


def shards(factor, pattern, owner, right_side):
    full = lax.all_gather(factor, "rhs", axis=1, tiled=True)
    order = lax.all_gather(owner, "rows", axis=0, tiled=True)
    total = order.shape[0]
    slots_dev = owner.shape[0]
    rows_dev = full.shape[0]
    width = full.shape[1]
    block = rows_dev // slots_dev
    leaf = total // 12
    third = width // 3
    third_blocks = total // 3
    inverse = jnp.zeros((total,), jnp.int32).at[order].set(jnp.arange(total, dtype=jnp.int32))
    level_own, group_own = classify(owner, leaf)
    level_col, group_col = classify(jnp.arange(total, dtype=jnp.int32), leaf)
    desc = (level_own[:, None] == 1) & (level_col[None, :] == 2) & (
        group_col[None, :] // 2 == group_own[:, None]
    ) | (level_own[:, None] == 0) & (level_col[None, :] > 0)
    same = (level_own[:, None] == level_col[None, :]) & (group_own[:, None] == group_col[None, :])
    keep_blocks = desc & (pattern > 0) | same
    row_index = (owner[:, None] * block + jnp.arange(block, dtype=jnp.int32)[None, :]).reshape(
        rows_dev
    )
    row_four = row_index.reshape(slots_dev, block, 1, 1)
    full_four = full.reshape(slots_dev, block, total, block)
    pieces = []
    for k in range(3):
        lower = k * third_blocks
        upper = lower + third_blocks
        col_four = (k * third + jnp.arange(third, dtype=jnp.int32)).reshape(
            1, 1, third_blocks, block
        )
        keep_four = keep_blocks[:, lower:upper][:, None, :, None]
        same_four = same[:, lower:upper][:, None, :, None]
        allowed = keep_four & (jnp.logical_not(same_four) | (row_four > col_four))
        pieces.append(
            jnp.where(allowed, full_four[:, :, lower:upper, :], 0.0).reshape(rows_dev, third)
        )
    level_rows = jnp.repeat(level_own, block)
    count = right_side.shape[0]
    solved = jnp.zeros((count, rows_dev), jnp.float32)
    update = jnp.zeros((count, rows_dev), jnp.float32)
    for lvl in (2, 1, 0):
        k = 2 - lvl
        resid = jnp.where(level_rows[None, :] == lvl, right_side - update, 0.0)
        whole = reorder(lax.all_gather(resid, "rows", axis=1, tiled=True), inverse, block)
        fresh = times_rows(whole[:, k * third : (k + 1) * third], pieces[k]) + resid
        solved = jnp.where(level_rows[None, :] == lvl, fresh, solved)
        if lvl > 0:
            carried = reorder(lax.all_gather(solved, "rows", axis=1, tiled=True), inverse, block)
            update = times_rows(carried[:, 0:third], pieces[0])
            for other in range(1, k + 1):
                update = update + times_rows(
                    carried[:, other * third : (other + 1) * third], pieces[other]
                )
    result = jnp.zeros((count, rows_dev), jnp.float32)
    pending = jnp.zeros((count, rows_dev), jnp.float32)
    for lvl in (0, 1, 2):
        k = 2 - lvl
        tvec = jnp.where(level_rows[None, :] == lvl, solved - pending, 0.0)
        outputs = [
            times_cols(tvec, pieces[j]) if j <= k else jnp.zeros((count, third), jnp.float32)
            for j in range(3)
        ]
        back = jnp.concatenate(outputs, axis=1)
        gotten = (
            lax.psum_scatter(reorder(back, order, block), "rows", scatter_dimension=1, tiled=True)
            + tvec
        )
        result = jnp.where(level_rows[None, :] == lvl, gotten, result)
        if lvl < 2:
            finished = jnp.where(level_rows[None, :] == lvl, result, 0.0)
            outputs = [
                (
                    times_cols(finished, pieces[j])
                    if j <= k
                    else jnp.zeros((count, third), jnp.float32)
                )
                for j in range(3)
            ]
            term = jnp.concatenate(outputs, axis=1)
            pending = pending + lax.psum_scatter(
                reorder(term, order, block), "rows", scatter_dimension=1, tiled=True
            )
    return result


def solution(mesh):
    in_specs = (P("rows", "rhs"), P("rows", None), P("rows"), P("rhs", "rows"))
    out_specs = P("rhs", "rows")
    return jax.shard_map(shards, mesh=mesh, in_specs=in_specs, out_specs=out_specs, check_vma=False)
```

profile of v0, /device:TPU:8, one launch (start us, length us, event | category | flops | bytes accessed | tf_op | source)
XLA Modules:
  0.0 1297.5 jit_solution(5779701427989357457)
XLA Ops:
  7.5 53.5 %all-gather = f32[64,192,16]{1,2,0:T(8,128)S(1)} all-gather(f32[1,192,16]{1,2,0:T(8,128)S(1)} %select_bitcast_fusion.10), channel_id=1, replica_groups=mesh['rows'=64,'rhs'=4] {'rows'}, dimensions={0}, use_global_device_ids=true | all-gather | bytes 798720 | tf_op jit(solution)/shard_map/all_gather | solution.py:74
  67.2 18.3 %all-reduce.1 = s32[192]{0:T(256)S(1)} all-reduce(s32[192]{0:T(256)S(1)} %dynamic-update-slice), channel_id=1, replica_groups=mesh['rows'=64,'rhs'=4] {'rows'}, use_global_device_ids=true, to_apply=%add.1 | all-reduce | flops 192 | bytes 1536
  91.1 15.5 %all-gather.7.cloned.1.call-done = f32[192,12288]{1,0:T(8,128)} async-done(((f32[192,3072]{1,0:T(8,128)}), f32[192,12288]{1,0:T(8,128)}) %all-gather.7.cloned.1.call-update) | async-done | bytes 9437200 | tf_op jit(solution)/shard_map/all_gather | solution.py:31
  106.6 15.6 %reshape.267 = f32[3,64,192,64]{3,2,1,0:T(8,128)} reshape(f32[192,12288]{1,0:T(8,128)} %all-gather.7.cloned.1.call-done) | data formatting | bytes 18874368 | tf_op jit(solution)/shard_map/reshape | solution.py:53
  122.3 14.7 %slice_select_fusion.1 = (f32[3,64,64,64]{3,2,1,0:T(8,128)}, f32[3,64,64,64]{3,2,1,0:T(8,128)}, f32[3,64,64,64]{3,2,1,0:T(8,128)}) fusion(f32[3,64,192,64]{3,2,1,0:T(8,128)} %reshape.267, s32[64,64]{1,0:T(8,128)S(1)} %fusion.14, s32[3,64]{1,0:T(4,128)S(1)} %iota_add_fusion.1, pred[3,64]{1,0:T(4,128)(4,1)S(1)} %get-tuple-element.16, ...), kind=kLoop, calls=%fused_computation.12 | loop fusion | flops 9437184 | bytes 18925440 | tf_op jit(solution)/shard_map/jit(_where)/select_n | solution.py:65
  137.0 4.5 reshape.268
  141.5 3.5 fusion.5
  145.0 51.5 %all-gather.1 = f32[64,192,16]{1,2,0:T(8,128)S(1)} all-gather(f32[1,192,16]{1,2,0:T(8,128)S(1)} %bitcast.108), channel_id=1, replica_groups=mesh['rows'=64,'rhs'=4] {'rows'}, dimensions={0}, use_global_device_ids=true | all-gather | bytes 798720 | tf_op jit(solution)/shard_map/all_gather | solution.py:78
  200.6 2.9 reshape.269
  203.5 3.5 copy.54
  207.0 3.3 gather_fusion.1
  216.4 3.5 fusion.4
  219.9 49.2 %all-gather.2 = f32[64,192,16]{1,2,0:T(8,128)S(1)} all-gather(f32[1,192,16]{1,2,0:T(8,128)S(1)} %bitcast.110), channel_id=1, replica_groups=mesh['rows'=64,'rhs'=4] {'rows'}, dimensions={0}, use_global_device_ids=true | all-gather | bytes 798720 | tf_op jit(solution)/shard_map/all_gather | solution.py:74
  276.2 3.5 copy.57
  279.6 3.3 gather_fusion.2
  289.1 5.9 reshape.273
  295.0 4.5 fusion.3
  299.5 48.9 %all-gather.3 = f32[64,192,16]{1,2,0:T(8,128)S(1)} all-gather(f32[1,192,16]{1,2,0:T(8,128)S(1)} %bitcast.107), channel_id=1, replica_groups=mesh['rows'=64,'rhs'=4] {'rows'}, dimensions={0}, use_global_device_ids=true | all-gather | bytes 798720 | tf_op jit(solution)/shard_map/all_gather | solution.py:78
  352.6 2.9 reshape.274
  355.5 3.5 copy.60
  359.0 3.3 gather_fusion.3
  368.4 3.6 fusion.8
  372.1 3.5 fusion.2
  375.6 49.2 %all-gather.4 = f32[64,192,16]{1,2,0:T(8,128)S(1)} all-gather(f32[1,192,16]{1,2,0:T(8,128)S(1)} %bitcast.109), channel_id=1, replica_groups=mesh['rows'=64,'rhs'=4] {'rows'}, dimensions={0}, use_global_device_ids=true | all-gather | bytes 798720 | tf_op jit(solution)/shard_map/all_gather | solution.py:74
  428.9 2.9 reshape.276
  431.8 3.5 copy.63
  435.3 3.3 gather_fusion.4
  444.7 6.0 reshape.278
  450.7 4.5 fusion
  461.6 2.9 reshape.279
  464.5 3.5 copy.65
  468.0 3.3 gather_fusion.5
  474.2 5.0 copy.85
  479.5 145.6 %reduce-scatter.16.cloned.1.call-done = f32[192,16]{1,0:T(8,128)} async-done(((f32[12288,16]{1,0:T(8,128)}), f32[192,16]{1,0:T(8,128)}) %reduce-scatter.16.cloned.1.call-update) | async-done | bytes 12304
  635.3 3.5 copy.67
  638.8 3.2 gather_fusion.6
  644.9 5.0 copy.86
  650.5 145.4 %reduce-scatter.18.cloned.1.call-done = f32[192,16]{1,0:T(8,128)} async-done(((f32[12288,16]{1,0:T(8,128)}), f32[192,16]{1,0:T(8,128)}) %reduce-scatter.18.cloned.1.call-update) | async-done | bytes 12304
  804.2 3.5 copy.69
  807.7 3.2 gather_fusion.7
  813.7 5.0 copy.87
  818.8 145.8 %reduce-scatter.20.cloned.1.call-done = f32[192,16]{1,0:T(8,128)} async-done(((f32[12288,16]{1,0:T(8,128)}), f32[192,16]{1,0:T(8,128)}) %reduce-scatter.20.cloned.1.call-update) | async-done | bytes 12304
  973.1 3.5 copy.71
  976.5 3.3 gather_fusion.8
  982.6 5.0 copy.88
  987.9 145.7 %reduce-scatter.22.cloned.1.call-done = f32[192,16]{1,0:T(8,128)} async-done(((f32[12288,16]{1,0:T(8,128)}), f32[192,16]{1,0:T(8,128)}) %reduce-scatter.22.cloned.1.call-update) | async-done | bytes 12304
  1138.9 4.0 copy.89
  1143.0 145.9 %reduce-scatter.24.cloned.1.call-done = f32[192,16]{1,0:T(8,128)} async-done(((f32[12288,16]{1,0:T(8,128)}), f32[192,16]{1,0:T(8,128)}) %reduce-scatter.24.cloned.1.call-update) | async-done | bytes 12304
  (132 shorter events, 108.3 us)
Async XLA Ops:
  6.5 0.8 copy-start.9
  6.5 1.0 copy-start.7
  6.5 100.1 %all-gather.7.cloned.1.call-start = ((), (), s32[]{:S(2)}) async-start(), calls=%async_computation.5 | async-start | bytes 11796480 | tf_op jit(solution)/shard_map/all_gather | solution.py:31
  7.3 617.8 %reduce-scatter.16.cloned.1.call-start = ((), (), s32[]{:S(2)}) async-start(), calls=%async_computation.6 | async-start | bytes 6389760
  64.7 0.9 copy-start.10
  89.0 1.9 copy-start.8
  368.4 3.6 copy-start
  455.3 1.9 copy-start.1
  457.2 1.9 copy-start.5
  479.2 316.6 %reduce-scatter.18.cloned.1.call-start = ((), (), s32[]{:S(2)}) async-start(), calls=%async_computation.7 | async-start | bytes 6389760
  626.1 1.9 copy-start.2
  628.0 1.9 copy-start.6
  649.9 314.8 %reduce-scatter.20.cloned.1.call-start = ((), (), s32[]{:S(2)}) async-start(), calls=%async_computation.8 | async-start | bytes 6389760
  796.8 1.9 copy-start.3
  818.8 314.8 %reduce-scatter.22.cloned.1.call-start = ((), (), s32[]{:S(2)}) async-start(), calls=%async_computation.9 | async-start | bytes 6389760
  965.7 1.9 copy-start.4
  987.7 301.2 %reduce-scatter.24.cloned.1.call-start = ((), (), s32[]{:S(2)}) async-start(), calls=%async_computation.10 | async-start | bytes 6389760
Sparse Core Ops, SparseCore 0:
  9.2 97.4 all-gather.6
  479.4 145.7 reduce-scatter.15
  650.1 145.7 reduce-scatter.17
  818.9 145.7 reduce-scatter.19
  987.8 145.7 reduce-scatter.21
  1143.1 145.7 reduce-scatter.23
where the time goes:
time: 1310 us; the launch traced here: 1300 us
  waiting for transfers between devices  745 us (57%)
  blocking collectives  271 us (21%)
  local copies, waits for them, and re-layouts  187 us (14%)
  matrix products  40.7 us (3%)
  other arithmetic  38.2 us (3%)
  between operations  14.7 us (1%)
    unnamed x11, waiting for transfers between devices  729 us
    all_gather x3, blocking collectives, shards(): lax.all_gather(resid, 'rows', axis=1, tiled=True)  152 us
    all_gather x2, blocking collectives, shards(): lax.all_gather(solved, 'rows', axis=1, tiled=True)  100 us
    reshape x20, local copies, waits for them, and re-layouts, reorder(): vectors.reshape(count, -1, block)  55.5 us
    unnamed x39, local copies, waits for them, and re-layouts  43 us
    gather x10, local copies, waits for them, and re-layouts, reorder(): jnp.take(vectors.reshape(count, -1, block), index, axis=1)  28 us
  transfers between devices with their start and end apart: 6, of which 6 were waited for; matrix products, arithmetic and copies ran while one was open for 1% of the time, Pallas kernels for 0%

commit v1 on v0

v1 whole, which is shorter than its diff:
```python
import functools

import jax
import jax.numpy as jnp
from jax import lax
from jax.experimental import pallas as pl
from jax.experimental.pallas import tpu as pltpu
from jax.sharding import Mesh, PartitionSpec as P

BLOCK = 64
RHS = 16
SLOTS = 3
ROWS = SLOTS * BLOCK
THIRD = 4096
PEERS = 32
PLACES = PEERS * SLOTS
VMEM = pl.BlockSpec(memory_space=pltpu.VMEM)
SMEM = pl.BlockSpec(memory_space=pltpu.SMEM)
PARAMS = pltpu.CompilerParams(vmem_limit_bytes=48 * 1024 * 1024)
CHIPS = ("x", "z")


def f32(*shape):
    return jax.ShapeDtypeStruct(shape, jnp.float32)


def classify(ids, leaf):
    level = jnp.where(ids < 4 * leaf, 2, jnp.where(ids < 8 * leaf, 1, 0)).astype(jnp.int32)
    group = jnp.where(
        level == 2, ids // leaf, jnp.where(level == 1, (ids - 4 * leaf) // (2 * leaf), 0)
    )
    return (level, group)


def left_half():
    return lax.broadcasted_iota(jnp.int32, (8, 128), 1) < BLOCK


def pack(rows):
    return [
        jnp.concatenate(
            [rows[:8, s * BLOCK : (s + 1) * BLOCK], rows[8:, s * BLOCK : (s + 1) * BLOCK]], axis=1
        )
        for s in range(SLOTS)
    ]


def unpack(tiles):
    upper = jnp.concatenate([t[:, :BLOCK] for t in tiles], axis=1)
    lower = jnp.concatenate([t[:, BLOCK:] for t in tiles], axis=1)
    return jnp.concatenate([upper, lower], axis=0)


def only(own_ref, level, rows):
    slot = lax.broadcasted_iota(jnp.int32, rows.shape, 1) // BLOCK
    keep = jnp.zeros(rows.shape, jnp.bool_)
    for s in range(SLOTS):
        g = own_ref[s]
        here = (g >= (2 - level) * 64) & (g < (3 - level) * 64)
        keep = keep | ((slot == s) & here)
    return jnp.where(keep, rows, 0.0)


def to_canonical(inv_ref, level, mine_ref, other_ref, x_ref):
    base = (2 - level) * 64
    half = left_half()

    def tile(place):
        far = place >= PLACES
        near_at = jnp.where(far, 0, place)
        far_at = jnp.where(far, place - PLACES, 0)
        chip, slot = near_at // SLOTS, near_at % SLOTS
        chip2, slot2 = far_at // SLOTS, far_at % SLOTS
        return jnp.where(far, other_ref[chip2, slot2], mine_ref[chip, slot])

    for t in range(32):
        a = tile(inv_ref[base + 2 * t])
        b = tile(inv_ref[base + 2 * t + 1])
        ra = pltpu.roll(a, BLOCK, 1)
        rb = pltpu.roll(b, BLOCK, 1)
        x_ref[0:8, 128 * t : 128 * (t + 1)] = jnp.where(half, a, rb)
        x_ref[8:16, 128 * t : 128 * (t + 1)] = jnp.where(half, ra, b)


def to_places(inv_ref, level, x_ref, out_ref):
    base = (2 - level) * 64
    half = left_half()
    out_ref[...] = jnp.zeros_like(out_ref)
    for t in range(32):
        top = x_ref[0:8, 128 * t : 128 * (t + 1)]
        bottom = x_ref[8:16, 128 * t : 128 * (t + 1)]
        out_ref[inv_ref[base + 2 * t]] = jnp.where(half, top, pltpu.roll(bottom, BLOCK, 1))
        out_ref[inv_ref[base + 2 * t + 1]] = jnp.where(half, pltpu.roll(top, BLOCK, 1), bottom)


def times_rows(x, m_ref):
    return lax.dot_general(
        x,
        m_ref[...],
        (((1,), (1,)), ((), ())),
        precision=lax.Precision.HIGHEST,
        preferred_element_type=jnp.float32,
    )


def times_cols(x, m_ref):
    return lax.dot_general(
        x,
        m_ref[...],
        (((1,), (0,)), ((), ())),
        precision=lax.Precision.HIGHEST,
        preferred_element_type=jnp.float32,
    )


def spread(tiles, send_ref):
    for peer in range(PEERS):
        for s in range(SLOTS):
            send_ref[peer, s] = tiles[s]


def arrived(got_ref):
    return unpack([jnp.sum(got_ref[:, s], axis=0) for s in range(SLOTS)])


def start_kernel(own_ref, b_ref, send_ref):
    tiles = pack(b_ref[...])
    lane = lax.broadcasted_iota(jnp.int32, (8, 128), 1)
    names = jnp.zeros((8, 128), jnp.float32)
    for s in range(SLOTS):
        names = jnp.where(lane == s, own_ref[s].astype(jnp.float32), names)
    spread(tiles, send_ref)
    for peer in range(PEERS):
        send_ref[peer, SLOTS] = names


def mask_kernel(own_ref, kind_ref, full_ref, out_ref):
    s = pl.program_id(0)
    col0 = pl.program_id(1) * out_ref.shape[1]
    g = own_ref[s]
    row = g * BLOCK + lax.broadcasted_iota(jnp.int32, out_ref.shape, 0)
    col = col0 + lax.broadcasted_iota(jnp.int32, out_ref.shape, 1)
    kind = kind_ref[0]
    allowed = (kind == 1) | ((kind == 2) & (row > col))
    out_ref[...] = jnp.where(allowed, full_ref[...], 0.0)


def leaves_kernel(own_ref, order_ref, b_ref, mine_ref, other_ref, m_ref, inv_ref, y_ref, send_ref, x_ref):
    def note(p, carry):
        inv_ref[order_ref[p]] = p
        return carry

    lax.fori_loop(0, 2 * PLACES, note, 0)
    to_canonical(inv_ref, 2, mine_ref, other_ref, x_ref)
    y = only(own_ref, 2, times_rows(x_ref[...], m_ref) + b_ref[...])
    y_ref[...] = y
    spread(pack(y), send_ref)


def resid_kernel(level, own_ref, inv_ref, b_ref, old_ref, mine_ref, other_ref, m_ref, upd_ref, r_ref, send_ref, x_ref):
    to_canonical(inv_ref, level + 1, mine_ref, other_ref, x_ref)
    upd = times_rows(x_ref[...], m_ref)
    if level == 0:
        upd = upd + old_ref[...]
    upd_ref[...] = upd
    r = only(own_ref, level, b_ref[...] - upd)
    r_ref[...] = r
    spread(pack(r), send_ref)


def middle_kernel(own_ref, inv_ref, r_ref, mine_ref, other_ref, m_ref, y_ref, send_ref, x_ref):
    to_canonical(inv_ref, 1, mine_ref, other_ref, x_ref)
    y = only(own_ref, 1, times_rows(x_ref[...], m_ref)) + r_ref[...]
    y_ref[...] = y
    spread(pack(y), send_ref)


def top_kernel(own_ref, inv_ref, r_ref, mine_ref, other_ref, m_ref, y_ref, part_ref, x_ref):
    to_canonical(inv_ref, 0, mine_ref, other_ref, x_ref)
    y = only(own_ref, 0, times_rows(x_ref[...], m_ref)) + r_ref[...]
    y_ref[...] = y
    x_ref[...] = times_cols(y, m_ref)
    to_places(inv_ref, 0, x_ref, part_ref)


def add_kernel(level, inv_ref, y_ref, got_ref, m_ref, x_out_ref, part_ref, x_ref):
    x = y_ref[...] + arrived(got_ref)
    x_out_ref[...] = x
    x_ref[...] = times_cols(x, m_ref)
    to_places(inv_ref, level, x_ref, part_ref)


def add_both_kernel(level, inv_ref, y_ref, other_x_ref, got_ref, m_ref, x_out_ref, part_ref, x_ref):
    x = y_ref[...] + arrived(got_ref) + other_x_ref[...]
    x_out_ref[...] = x
    x_ref[...] = times_cols(x, m_ref)
    to_places(inv_ref, level, x_ref, part_ref)


def sub_kernel(level, own_ref, inv_ref, y_ref, got_ref, m_ref, t_ref, part_ref, x_ref):
    t = only(own_ref, level, y_ref[...] - arrived(got_ref))
    t_ref[...] = t
    x_ref[...] = times_cols(t, m_ref)
    to_places(inv_ref, level, x_ref, part_ref)


def last_kernel(t_ref, x_ref, got_ref, out_ref):
    out_ref[...] = t_ref[...] + x_ref[...] + arrived(got_ref)


def swap(x):
    return lax.ppermute(x, "c", [(0, 1), (1, 0)])


def exchange(x):
    return lax.all_to_all(x, CHIPS, 0, 0)


def gather(send):
    mine = exchange(send)
    return mine, swap(mine)


def reduce(part):
    far = swap(part[PLACES:])
    return exchange((part[:PLACES] + far).reshape(PEERS, SLOTS, 8, 128))


def call(kernel, outs, specs, out_specs, scratch=True):
    return pl.pallas_call(
        kernel,
        out_shape=outs,
        in_specs=specs,
        out_specs=out_specs,
        scratch_shapes=[pltpu.VMEM((RHS, THIRD), jnp.float32)] if scratch else [],
        compiler_params=PARAMS,
    )


def shards(factor, pattern, owner, right_side):
    total = pattern.shape[1]
    leaf = total // 12
    width = total * BLOCK
    vec = f32(RHS, ROWS)
    send_shape = f32(PEERS, SLOTS, 8, 128)
    part_shape = f32(2 * PLACES, 8, 128)

    full = lax.all_gather(factor, "y", axis=1, tiled=True)

    send = call(start_kernel, f32(PEERS, SLOTS + 1, 8, 128), [SMEM, VMEM], VMEM, False)(owner, right_side)
    mine, other = gather(send)
    names = jnp.concatenate([mine[:, SLOTS, 0, :SLOTS], other[:, SLOTS, 0, :SLOTS]], axis=0)
    order = names.reshape(-1).astype(jnp.int32)

    level_own, group_own = classify(owner, leaf)
    level_col, group_col = classify(jnp.arange(total, dtype=jnp.int32), leaf)
    desc = (level_own[:, None] == 1) & (level_col[None, :] == 2) & (
        group_col[None, :] // 2 == group_own[:, None]
    ) | (level_own[:, None] == 0) & (level_col[None, :] > 0)
    same = (level_own[:, None] == level_col[None, :]) & (group_own[:, None] == group_col[None, :])
    kind = jnp.where(same, 2, jnp.where(desc & (pattern > 0), 1, 0)).astype(jnp.int32)
    kind = jnp.broadcast_to(kind[:, :, None], (SLOTS, total, BLOCK)).reshape(SLOTS, 1, width)

    def masked(k):
        tile = 2048
        per = THIRD // tile

        def kernel(own_ref, kind_ref, full_ref, out_ref):
            s = pl.program_id(0)
            col0 = k * THIRD + pl.program_id(1) * tile
            row = own_ref[s] * BLOCK + lax.broadcasted_iota(jnp.int32, out_ref.shape, 0)
            col = col0 + lax.broadcasted_iota(jnp.int32, out_ref.shape, 1)
            kinds = kind_ref[0]
            allowed = (kinds == 1) | ((kinds == 2) & (row > col))
            out_ref[...] = jnp.where(allowed, full_ref[...], 0.0)

        return pl.pallas_call(
            kernel,
            grid=(SLOTS, per),
            out_shape=f32(ROWS, THIRD),
            in_specs=[
                SMEM,
                pl.BlockSpec((1, 1, tile), lambda s, j: (s, 0, k * per + j)),
                pl.BlockSpec((BLOCK, tile), lambda s, j: (s, k * per + j)),
            ],
            out_specs=pl.BlockSpec((BLOCK, tile), lambda s, j: (s, j)),
            compiler_params=PARAMS,
        )(owner, kind, full)

    m2, m1, m0 = masked(0), masked(1), masked(2)

    inv, y2, send = call(
        leaves_kernel,
        (jax.ShapeDtypeStruct((total,), jnp.int32), vec, send_shape),
        [SMEM, SMEM, VMEM, VMEM, VMEM, VMEM],
        (SMEM, VMEM, VMEM),
    )(owner, order, right_side, mine, other, m2)
    mine, other = gather(send)
    upd, r1, send = call(
        functools.partial(resid_kernel, 1),
        (vec, vec, send_shape),
        [SMEM, SMEM] + [VMEM] * 5,
        (VMEM, VMEM, VMEM),
    )(owner, inv, right_side, right_side, mine, other, m2)
    mine, other = gather(send)
    y1, send = call(
        middle_kernel, (vec, send_shape), [SMEM, SMEM] + [VMEM] * 4, (VMEM, VMEM)
    )(owner, inv, r1, mine, other, m1)
    mine, other = gather(send)
    upd, r0, send = call(
        functools.partial(resid_kernel, 0),
        (vec, vec, send_shape),
        [SMEM, SMEM] + [VMEM] * 5,
        (VMEM, VMEM, VMEM),
    )(owner, inv, right_side, upd, mine, other, m1)
    mine, other = gather(send)
    y0, part = call(
        top_kernel, (vec, part_shape), [SMEM, SMEM] + [VMEM] * 4, (VMEM, VMEM)
    )(owner, inv, r0, mine, other, m0)

    got = reduce(part)
    x0, part = call(
        functools.partial(add_kernel, 1), (vec, part_shape), [SMEM] + [VMEM] * 3, (VMEM, VMEM)
    )(inv, y0, got, m1)
    got = reduce(part)
    t1, part = call(
        functools.partial(sub_kernel, 1), (vec, part_shape), [SMEM, SMEM] + [VMEM] * 3, (VMEM, VMEM)
    )(owner, inv, y1, got, m1)
    got = reduce(part)
    x01, part = call(
        functools.partial(add_both_kernel, 2), (vec, part_shape), [SMEM] + [VMEM] * 4, (VMEM, VMEM)
    )(inv, t1, x0, got, m2)
    got = reduce(part)
    t2, part = call(
        functools.partial(sub_kernel, 2), (vec, part_shape), [SMEM, SMEM] + [VMEM] * 3, (VMEM, VMEM)
    )(owner, inv, y2, got, m2)
    got = reduce(part)
    return call(last_kernel, vec, [VMEM] * 3, VMEM, False)(t2, x01, got)


def solution(mesh):
    fine = Mesh(mesh.devices.reshape(4, 8, 2, 4), ("x", "z", "c", "y"))
    rows = ("x", "z", "c")
    in_specs = (P(rows, "y"), P(rows, None), P(rows), P("y", rows))
    out_specs = P("y", rows)
    return jax.shard_map(shards, mesh=fine, in_specs=in_specs, out_specs=out_specs, check_vma=False)
```

time: 1310 us -> 356 us (0.27)
  waiting for transfers between devices: 745 us -> 96.5 us
  local copies, waits for them, and re-layouts: 187 us -> 2.3 us
  blocking collectives: 271 us -> 182 us
  Pallas kernels: 0 us -> 46.7 us
  matrix products: 40.7 us -> 0 us
  other arithmetic: 38.2 us -> 0.46 us
    unnamed x11 -> x1, waiting for transfers between devices: 729 us -> 0.71 us
    all_gather x5 -> x0, blocking collectives: 252 us -> none  [the longest x3 152 us: shards(): lax.all_gather(resid, 'rows', axis=1, tiled=True)]
    all_to_all x0 -> x9, blocking collectives: none -> 182 us  [exchange(): return lax.all_to_all(x, CHIPS, 0, 0)]
    reshape x29 -> x1, local copies, waits for them, and re-layouts: 100 us -> 0.2 us  [shards(): jnp.broadcast_to(kind[:, :, None], (SLOTS, total, BLOCK))]
    all_gather x1, waiting for transfers between devices: 15.5 us -> 66 us  [shards(): full = lax.all_gather(factor, 'y', axis=1, tiled=True)]
    pallas_call x0 -> x14, Pallas kernels: none -> 46.7 us  [the longest x3 12.1 us: masked(): pl.pallas_call(kernel, grid=(SLOTS, per), out_shape=f32(ROWS, THIRD), in_...]
    unnamed x39 -> x10, local copies, waits for them, and re-layouts: 43 us -> 1.38 us
    dot_general x17 -> x0, matrix products: 40.7 us -> none  [the longest x6 23.2 us: times_rows(): lax.dot_general(vectors, matrix, (((1,), (1,)), ((), ())), precision=lax....]
  transfers between devices with their start and end apart: 6 -> 12, of which waited for: 6 -> 10; matrix products, arithmetic and copies ran while one was open for 1% -> 0% of each run, Pallas kernels for 0% -> 3%
where the time goes in v1:
time: 356 us; the launch traced here: 355 us
  blocking collectives  182 us (51%)
  waiting for transfers between devices  96.5 us (27%)
  Pallas kernels  46.7 us (13%)
  between operations  13.7 us (4%)
  starting transfers between devices  12.5 us (4%)
    all_to_all x9, blocking collectives, exchange(): return lax.all_to_all(x, CHIPS, 0, 0)  182 us
    all_gather x1, waiting for transfers between devices, shards(): full = lax.all_gather(factor, 'y', axis=1, tiled=True)  66 us
    all_to_all x1, waiting for transfers between devices, exchange(): return lax.all_to_all(x, CHIPS, 0, 0)  16.8 us
    ppermute x10, waiting for transfers between devices, swap(): return lax.ppermute(x, 'c', [(0, 1), (1, 0)])  13 us
    pallas_call x3, Pallas kernels, masked(): pl.pallas_call(kernel, grid=(SLOTS, per), out_shape=f32(ROWS, THIRD), in_...  12.1 us
    all_to_all x1, starting transfers between devices, exchange(): return lax.all_to_all(x, CHIPS, 0, 0)  11.3 us
  transfers between devices with their start and end apart: 12, of which 10 were waited for; matrix products, arithmetic and copies ran while one was open for 0% of the time, Pallas kernels for 3%

profile of v1, /device:TPU:8, one launch (start us, length us, event | category | flops | bytes accessed | tf_op | source)
XLA Modules:
  0.0 354.5 jit_solution(8189554793414282735)
XLA Ops:
  6.5 0.7 all-gather.2.cloned.1.call-update
  7.3 0.7 copy-done
  8.0 0.7 copy-done.2
  8.6 1.4 shard_map.46
  10.1 11.3 %all-to-all-start = ((f32[32,4,8,128]{3,2,1,0:T(8,128)}), f32[32,4,8,128]{3,2,1,0:T(8,128)S(1)}, u32[]{:S(2)}, u32[]{:S(2)}) async-start(f32[32,4,8,128]{3,2,1,0:T(8,128)} %shard_map.46), calls=%async_computation | async-start | bytes 1048576 | tf_op jit(solution)/shard_map/all_to_all | solution.py:216
  21.5 16.8 %all-to-all-done.mine_ref = f32[32,4,8,128]{3,2,1,0:T(8,128)S(1)} async-done(((f32[32,4,8,128]{3,2,1,0:T(8,128)}), f32[32,4,8,128]{3,2,1,0:T(8,128)S(1)}, u32[]{:S(2)}, u32[]{:S(2)}) %all-to-all-start) | async-done | bytes 524320 | tf_op jit(solution)/shard_map/all_to_all | solution.py:216
  38.3 0.1 select_select_fusion
  38.4 0.1 broadcast_in_dim.62
  38.5 0.2 reshape.119.kind_ref
  38.8 1.3 collective-permute-done.other_ref
  40.3 0.1 maximum_convert_fusion
  40.4 0.1 copy.9
  40.5 0.1 convert_element_type.6.order_ref
  40.6 66.0 %all-gather.2.cloned.1.call-done.full_ref = f32[192,12288]{1,0:T(8,128)} async-done(((f32[192,3072]{1,0:T(8,128)}), f32[192,12288]{1,0:T(8,128)}) %all-gather.2.cloned.1.call-update) | async-done | bytes 9437200 | tf_op jit(solution)/shard_map/all_gather | solution.py:248
  106.6 4.0 %shard_map.47.m_ref = f32[192,4096]{1,0:T(8,128)S(1)} custom-call(s32[3]{0:T(128)S(1)} %copy-done.3, s32[3,1,12288]{2,1,0:T(1,128)S(1)} %reshape.119.kind_ref, f32[192,12288]{1,0:T(8,128)} %all-gather.2.cloned.1.call-done.full_ref), custom_call_target="tpu_custom_call" | custom-call | tf_op jit(solution)/shard_map/pallas_call | solution.py:277
  110.7 5.5 %shard_map.48 = (s32[192]{0:T(256)S(1)}, f32[16,192]{1,0:T(8,128)S(1)}, f32[32,3,8,128]{3,2,1,0:T(8,128)S(1)}) custom-call(s32[3]{0:T(128)S(1)} %copy-done.3, s32[192]{0:T(256)S(1)} %convert_element_type.6.order_ref, f32[16,192]{1,0:T(8,128)S(1)} %copy-done.1, f32[32,4,8,128]{3,2,1,0:T(8,128)S(1)} %all-to-all-done.mine_ref, ...), custom_call_target="tpu_custom_call" | custom-call | tf_op jit(solution)/shard_map/pallas_call | solution.py:292
  116.2 24.1 %all_to_all.50.mine_ref = f32[32,3,8,128]{3,2,1,0:T(8,128)S(1)} all-to-all(f32[32,3,8,128]{3,2,1,0:T(8,128)S(1)} %get-tuple-element.27), channel_id=1, replica_groups=mesh['x'=4,'z'=8,'c'=2,'y'=4] {'x','z'}, dimensions={0} | all-to-all | bytes 786432 | tf_op jit(solution)/shard_map/all_to_all | solution.py:216
  140.3 1.7 collective-permute-done.1.other_ref
  142.0 3.6 %shard_map.49 = (f32[16,192]{1,0:T(8,128)S(1)}, f32[16,192]{1,0:T(8,128)S(1)}, f32[32,3,8,128]{3,2,1,0:T(8,128)S(1)}) custom-call(s32[3]{0:T(128)S(1)} %copy-done.3, s32[192]{0:T(256)S(1)} %get-tuple-element.25.inv_ref, f32[16,192]{1,0:T(8,128)S(1)} %copy-done.1, f32[16,192]{1,0:T(8,128)S(1)} %copy-done.1, f32[32,3,8,128]{3,2,1,0:T(8,128)S(1)} %all_to_all.50.mine_ref, ...), custom_call_target="tpu_custom_call" | custom-call | tf_op jit(solution)/shard_map/pallas_call | solution.py:299
  145.6 19.3 %all_to_all.51.mine_ref = f32[32,3,8,128]{3,2,1,0:T(8,128)S(1)} all-to-all(f32[32,3,8,128]{3,2,1,0:T(8,128)S(1)} %get-tuple-element.29), channel_id=1, replica_groups=mesh['x'=4,'z'=8,'c'=2,'y'=4] {'x','z'}, dimensions={0} | all-to-all | bytes 786432 | tf_op jit(solution)/shard_map/all_to_all | solution.py:216
  164.9 4.0 %shard_map.50.m_ref = f32[192,4096]{1,0:T(8,128)S(1)} custom-call(s32[3]{0:T(128)S(1)} %copy-done.3, s32[3,1,12288]{2,1,0:T(1,128)S(1)} %reshape.119.kind_ref, f32[192,12288]{1,0:T(8,128)} %all-gather.2.cloned.1.call-done.full_ref), custom_call_target="tpu_custom_call" | custom-call | tf_op jit(solution)/shard_map/pallas_call | solution.py:277
  169.0 3.6 %shard_map.51 = (f32[16,192]{1,0:T(8,128)S(1)}, f32[32,3,8,128]{3,2,1,0:T(8,128)S(1)}) custom-call(s32[3]{0:T(128)S(1)} %copy-done.3, s32[192]{0:T(256)S(1)} %get-tuple-element.25.inv_ref, f32[16,192]{1,0:T(8,128)S(1)} %get-tuple-element.28.r_ref, f32[32,3,8,128]{3,2,1,0:T(8,128)S(1)} %all_to_all.51.mine_ref, ...), custom_call_target="tpu_custom_call" | custom-call | tf_op jit(solution)/shard_map/pallas_call | solution.py:306
  172.6 20.1 %all_to_all.52.mine_ref = f32[32,3,8,128]{3,2,1,0:T(8,128)S(1)} all-to-all(f32[32,3,8,128]{3,2,1,0:T(8,128)S(1)} %get-tuple-element.32), channel_id=1, replica_groups=mesh['x'=4,'z'=8,'c'=2,'y'=4] {'x','z'}, dimensions={0} | all-to-all | bytes 786432 | tf_op jit(solution)/shard_map/all_to_all | solution.py:216
  192.7 1.7 collective-permute-done.3.other_ref
  194.4 4.1 %shard_map.52 = (f32[16,192]{1,0:T(8,128)}, f32[16,192]{1,0:T(8,128)S(1)}, f32[32,3,8,128]{3,2,1,0:T(8,128)S(1)}) custom-call(s32[3]{0:T(128)S(1)} %copy-done.3, s32[192]{0:T(256)S(1)} %get-tuple-element.25.inv_ref, f32[16,192]{1,0:T(8,128)S(1)} %copy-done.1, f32[16,192]{1,0:T(8,128)S(1)} %get-tuple-element.31.old_ref, ...), custom_call_target="tpu_custom_call" | custom-call | tf_op jit(solution)/shard_map/pallas_call | solution.py:310
  198.5 19.8 %all_to_all.53.mine_ref = f32[32,3,8,128]{3,2,1,0:T(8,128)S(1)} all-to-all(f32[32,3,8,128]{3,2,1,0:T(8,128)S(1)} %get-tuple-element.34), channel_id=1, replica_groups=mesh['x'=4,'z'=8,'c'=2,'y'=4] {'x','z'}, dimensions={0} | all-to-all | bytes 786432 | tf_op jit(solution)/shard_map/all_to_all | solution.py:216
  218.3 4.0 %shard_map.53.m_ref = f32[192,4096]{1,0:T(8,128)S(1)} custom-call(s32[3]{0:T(128)S(1)} %copy-done.3, s32[3,1,12288]{2,1,0:T(1,128)S(1)} %reshape.119.kind_ref, f32[192,12288]{1,0:T(8,128)} %all-gather.2.cloned.1.call-done.full_ref), custom_call_target="tpu_custom_call" | custom-call | tf_op jit(solution)/shard_map/pallas_call | solution.py:277
  222.3 7.0 %shard_map.54 = (f32[16,192]{1,0:T(8,128)S(1)}, f32[192,8,128]{2,1,0:T(8,128)S(1)}) custom-call(s32[3]{0:T(128)S(1)} %copy-done.3, s32[192]{0:T(256)S(1)} %get-tuple-element.25.inv_ref, f32[16,192]{1,0:T(8,128)S(1)} %get-tuple-element.33.r_ref, f32[32,3,8,128]{3,2,1,0:T(8,128)S(1)} %all_to_all.53.mine_ref, ...), custom_call_target="tpu_custom_call" | custom-call | tf_op jit(solution)/shard_map/pallas_call | solution.py:317
  229.4 0.6 collective-permute-start.5
  230.0 1.3 collective-permute-done.5
  231.4 19.9 %all_to_all.54.got_ref = f32[32,3,8,128]{3,2,1,0:T(8,128)S(1)} all-to-all(f32[32,3,8,128]{3,2,1,0:T(8,128)S(1)} %bitcast.7), channel_id=1, replica_groups=mesh['x'=4,'z'=8,'c'=2,'y'=4] {'x','z'}, dimensions={0} | all-to-all | bytes 786432 | tf_op jit(solution)/shard_map/all_to_all | solution.py:216
  251.3 2.2 shard_map.55
  253.5 0.3 collective-permute-start.6
  253.8 1.7 collective-permute-done.6
  255.6 19.8 %all_to_all.55.got_ref = f32[32,3,8,128]{3,2,1,0:T(8,128)S(1)} all-to-all(f32[32,3,8,128]{3,2,1,0:T(8,128)S(1)} %bitcast.8), channel_id=1, replica_groups=mesh['x'=4,'z'=8,'c'=2,'y'=4] {'x','z'}, dimensions={0} | all-to-all | bytes 786432 | tf_op jit(solution)/shard_map/all_to_all | solution.py:216
  275.4 2.2 shard_map.56
  277.7 0.1 collective-permute-start.7
  277.8 1.7 collective-permute-done.7
  279.5 19.8 %all_to_all.56.got_ref = f32[32,3,8,128]{3,2,1,0:T(8,128)S(1)} all-to-all(f32[32,3,8,128]{3,2,1,0:T(8,128)S(1)} %bitcast.9), channel_id=1, replica_groups=mesh['x'=4,'z'=8,'c'=2,'y'=4] {'x','z'}, dimensions={0} | all-to-all | bytes 786432 | tf_op jit(solution)/shard_map/all_to_all | solution.py:216
  299.3 2.2 shard_map.57
  301.5 0.1 collective-permute-start.8
  301.6 1.7 collective-permute-done.8
  303.4 19.8 %all_to_all.57.got_ref = f32[32,3,8,128]{3,2,1,0:T(8,128)S(1)} all-to-all(f32[32,3,8,128]{3,2,1,0:T(8,128)S(1)} %bitcast.10), channel_id=1, replica_groups=mesh['x'=4,'z'=8,'c'=2,'y'=4] {'x','z'}, dimensions={0} | all-to-all | bytes 786432 | tf_op jit(solution)/shard_map/all_to_all | solution.py:216
  323.1 2.2 shard_map.58
  325.3 0.1 collective-permute-start.9
  325.4 1.7 collective-permute-done.9
  327.2 19.8 %all_to_all.58.got_ref = f32[32,3,8,128]{3,2,1,0:T(8,128)S(1)} all-to-all(f32[32,3,8,128]{3,2,1,0:T(8,128)S(1)} %bitcast.11), channel_id=1, replica_groups=mesh['x'=4,'z'=8,'c'=2,'y'=4] {'x','z'}, dimensions={0} | all-to-all | bytes 786432 | tf_op jit(solution)/shard_map/all_to_all | solution.py:216
  347.0 0.7 shard_map.59
  (35 shorter events, 0.7 us)
Async XLA Ops:
  6.5 14.9 %copy-start.3 = (s32[3]{0:T(128)S(1)}, s32[3]{0:T(128)}, u32[]{:S(2)}) copy-start(s32[3]{0:T(128)} %own_ref.21) | copy-start | bytes 40
  6.5 31.8 %copy-start.4 = (s32[3,192]{1,0:T(4,128)S(1)}, s32[3,192]{1,0:T(4,128)}, u32[]{:S(2)}) copy-start(s32[3,192]{1,0:T(4,128)} %param.5) | copy-start | bytes 6916
  6.5 100.1 %all-gather.2.cloned.1.call-start = ((), (), s32[]{:S(2)}) async-start(), calls=%async_computation.10 | async-start | bytes 11796480 | tf_op jit(solution)/shard_map/all_gather | solution.py:248
  7.3 0.7 copy-start
  8.0 0.7 copy-start.2
  10.1 28.2 %all-to-all-start = ((f32[32,4,8,128]{3,2,1,0:T(8,128)}), f32[32,4,8,128]{3,2,1,0:T(8,128)S(1)}, u32[]{:S(2)}, u32[]{:S(2)}) async-start(f32[32,4,8,128]{3,2,1,0:T(8,128)} %shard_map.46), calls=%async_computation | async-start | bytes 1048576 | tf_op jit(solution)/shard_map/all_to_all | solution.py:216
  38.3 1.9 collective-permute-start
  40.6 70.1 %copy-start.1 = (f32[16,192]{1,0:T(8,128)S(1)}, f32[16,192]{1,0:T(8,128)}, u32[]{:S(2)}) copy-start(f32[16,192]{1,0:T(8,128)} %b_ref.7) | copy-start | bytes 36868
  140.3 1.7 collective-permute-start.1
  164.9 4.1 %collective-permute-start.2 = (f32[32,3,8,128]{3,2,1,0:T(8,128)S(1)}, f32[32,3,8,128]{3,2,1,0:T(8,128)S(1)}, u32[]{:S(2)}, u32[]{:S(2)}) collective-permute-start(f32[32,3,8,128]{3,2,1,0:T(8,128)S(1)} %all_to_all.51.mine_ref), channel_id=1, source_target_pairs={{0,4},{4,0},{1,5},{5,1},{2,6},{6,2},{3,7},{7,3},{8,12},{12,8},{9,1... | collective-permute-start | bytes 1179656 | tf_op jit(solution)/shard_map/ppermute | solution.py:212
  192.7 1.7 collective-permute-start.3
  218.3 4.1 %collective-permute-start.4 = (f32[32,3,8,128]{3,2,1,0:T(8,128)S(1)}, f32[32,3,8,128]{3,2,1,0:T(8,128)S(1)}, u32[]{:S(2)}, u32[]{:S(2)}) collective-permute-start(f32[32,3,8,128]{3,2,1,0:T(8,128)S(1)} %all_to_all.53.mine_ref), channel_id=1, source_target_pairs={{0,4},{4,0},{1,5},{5,1},{2,6},{6,2},{3,7},{7,3},{8,12},{12,8},{9,1... | collective-permute-start | bytes 1179656 | tf_op jit(solution)/shard_map/ppermute | solution.py:212
  229.4 1.9 collective-permute-start.5
  253.5 2.0 collective-permute-start.6
  277.7 1.8 collective-permute-start.7
  301.5 1.8 collective-permute-start.8
  325.3 1.8 collective-permute-start.9
Sparse Core Ops, SparseCore 0:
  9.2 97.4 all-gather.1
